TPU v7x, 32 devices: a whole 2x2x4 slice. The times are simulated.
32 devices in a mesh: dim: 2 (over core), grp: 16 (over z, y, x).
Axes of the slice: x: 2, y: 2, z: 4, core: 2. Of those that a mesh axis runs over, the one named last changes fastest.
Arguments:
- states: bfloat16 [32768, 4096], P('grp', 'dim'), may hold values from -6 to 6
- pca: bfloat16 [4096, 1024], P('dim'), may hold values from -0.125 to 0.125
- centroids: float32 [256, 1024], P(None, 'dim'), may hold values from -3 to 3
- list_ids: int32 [32768, 1], P('grp'), may hold values from 0 to 255; in each aligned block of 2048 rows (0 to 2047, 2048 to 4095, ...) at most 16 rows name the same one
- prior_counts: int32 [256], P('grp'), may hold values from 1 to 63
- prior_gram: float32 [256, 1024, 1024], P('grp', 'dim'), may hold values from -96 to 96
Outputs:
- moments: float32 [256, 1024, 1024], P('grp', 'dim')
Inputs may be any that keep to these rules, and one draw needn't show every extreme that they name: `list_ids`: among the passages of one index of grp, no list is named by more than 16 passages, a bound that some block reaches.
All inputs are finite; a program needn't handle non-finite values.
Results may differ from a plain program's by a relative error of at most 0.0095.
Values may be sent and summed in bfloat16 or wider, within the bound.
A program may use at most 192 MiB of HBM per device.

v0:
```python
import jax
import jax.numpy as jnp
from jax import lax
from jax.sharding import PartitionSpec as P

LISTS = 256
MOST = 16


def on_device(states, pca, centroids, list_ids, prior_counts, prior_gram):
    own_width = prior_gram.shape[1]
    row_count = states.shape[0]
    projected_t = lax.psum_scatter(
        lax.dot_general(
            pca, states, (((0,), (1,)), ((), ())), preferred_element_type=jnp.float32
        ).astype(jnp.bfloat16),
        "dim",
        scatter_dimension=0,
        tiled=True,
    ).astype(jnp.float32)
    labels = list_ids[:, 0]
    onehot_int = (labels[None, :] == lax.broadcasted_iota(jnp.int32, (LISTS, row_count), 0)).astype(
        jnp.int32
    )
    onehot_t = onehot_int.astype(jnp.float32)
    shift_t = lax.dot_general(
        centroids,
        onehot_t,
        (((0,), (0,)), ((), ())),
        precision=lax.Precision.HIGHEST,
        preferred_element_type=jnp.float32,
    )
    residual_t = (projected_t - shift_t).astype(jnp.bfloat16)
    list_counts = jnp.sum(onehot_int, axis=1)
    earlier = jnp.cumsum(onehot_int, axis=1) - onehot_int
    ranks = jnp.sum(earlier * onehot_int, axis=0)
    slots = labels * MOST + ranks
    buffer = jnp.zeros((LISTS * MOST, own_width), jnp.bfloat16).at[slots].set(residual_t.T)
    buffer = buffer.reshape(LISTS, MOST, own_width)
    routed, got_counts = (
        lax.all_to_all(buffer, "grp", split_axis=0, concat_axis=1, tiled=True),
        lax.all_to_all(list_counts[:, None], "grp", split_axis=0, concat_axis=1, tiled=True),
    )
    new_gram = jnp.einsum(
        "lsa,lsb->lab",
        routed,
        lax.all_gather(routed, "dim", axis=2, tiled=True),
        preferred_element_type=jnp.float32,
    )
    new_counts = jnp.sum(got_counts, axis=1)
    totals = (prior_counts + new_counts).astype(jnp.float32)
    return (prior_gram + new_gram) / totals[:, None, None]


def solution(mesh):
    in_specs = (
        P("grp", "dim"),
        P("dim", None),
        P(None, "dim"),
        P("grp", None),
        P("grp"),
        P("grp", "dim", None),
    )
    out_specs = P("grp", "dim", None)
    return jax.shard_map(
        on_device, mesh=mesh, in_specs=in_specs, out_specs=out_specs, check_vma=False
    )
```

profile of v0, /device:TPU:0, one launch (start us, length us, event | category | flops | bytes accessed | tf_op | source)
XLA Modules:
  0.0 210.6 jit_solution(11961087361953576125)
XLA Ops:
  6.5 0.0 copy-start
  6.5 0.0 reduce-scatter.2.cloned.1.call-start
  6.5 13.9 %convolution_convert_fusion = bf16[1024,2048]{1,0:T(8,128)(2,1)} fusion(bf16[2048,1024]{1,0:T(8,128)(2,1)} %param.7, bf16[2048,2048]{1,0:T(8,128)(2,1)} %param.6), kind=kOutput, calls=%fused_computation.4 | convolution fusion | flops 8592031744 | bytes 16777216 | tf_op jit(solution)/shard_map/dot_general | solution.py:14
  20.5 0.0 copy-start.2
  20.5 0.0 reduce-scatter.2.cloned.1.call-update
  20.5 0.2 all-gather.2.cloned.1.call-start
  20.7 0.4 copy-done.2
  21.2 0.1 copy.29
  21.3 0.3 fusion.1
  21.7 2.7 %fusion.5 = s32[16,128]{0,1:T(8,128)S(1)} fusion(s32[256,16,128]{0,1,2:T(8,128)S(1)} %fusion.1, s32[256,16]{0,1:T(8,128)S(1)} %slice.9, s32[16,128]{0,1:T(8,128)S(1)} %copy.29), kind=kLoop, calls=%fused_computation.12 | loop fusion | flops 3143680 | bytes 2129920 | tf_op jit(solution)/shard_map/reduce_sum | solution.py:36
  24.4 0.1 copy.30
  24.5 10.9 %reduce-scatter.2.cloned.1.call-done = bf16[512,2048]{1,0:T(8,128)(2,1)} async-done(((bf16[1024,2048]{1,0:T(8,128)(2,1)}), bf16[512,2048]{1,0:T(8,128)(2,1)}) %reduce-scatter.2.cloned.1.call-update) | async-done | bytes 2097168 | tf_op jit(solution)/shard_map/reduce_scatter | solution.py:13
  35.4 0.0 copy-done
  35.4 5.3 %fusion.3 = bf16[2048,512]{0,1:T(8,128)(2,1)S(1)} fusion(f32[256,512]{1,0:T(8,128)S(1)} %copy-done, bf16[512,2048]{1,0:T(8,128)(2,1)} %reduce-scatter.2.cloned.1.call-done, s32[2048]{0:T(1024)S(1)} %bitcast.31), kind=kOutput, calls=%fused_computation.10 | convolution fusion | flops 3225944064 | bytes 4726784 | tf_op jit(solution)/shard_map/dot_general | solution.py:26
  40.7 2.5 %copy.32 = bf16[2048,512]{1,0:T(8,128)(2,1)} copy(bf16[2048,512]{0,1:T(8,128)(2,1)S(1)} %fusion.3) | data formatting | bytes 4194304 | tf_op jit(solution)/shard_map/transpose | solution.py:38
  43.2 12.6 %scatter_custom_fusion = bf16[4096,512]{1,0:T(8,128)(2,1)} fusion(s32[2048]{0:T(1024)S(1)} %bitcast.35, bf16[2048,512]{1,0:T(8,128)(2,1)} %copy.32, bf16[]{:T(256)} %constant.4.clone.1), kind=kCustom, calls=%fused_computation.15 | custom fusion | bytes 4194816 | tf_op jit(solution)/shard_map/scatter | solution.py:38
  55.9 101.0 %all_to_all.31 = bf16[256,16,512]{2,1,0:T(8,128)(2,1)S(1)} all-to-all(bf16[256,16,512]{2,1,0:T(8,128)(2,1)} %bitcast.28), channel_id=1, replica_groups=mesh['dim'=2,'grp'=16] {'grp'}, dimensions={0} | all-to-all | bytes 8388608 | tf_op jit(solution)/shard_map/all_to_all | solution.py:41
  156.9 2.4 %copy.33 = bf16[16,16,16,512]{3,2,1,0:T(8,128)(2,1)} copy(bf16[16,16,16,512]{3,2,0,1:T(8,128)(2,1)S(1)} %bitcast.29) | data formatting | bytes 8388608 | tf_op jit(solution)/shard_map/all_to_all | solution.py:41
  159.3 0.0 copy-start.3
  159.3 0.0 all-gather.2.cloned.1.call-update
  159.4 0.3 convert_reduce_fusion
  159.7 0.1 all_to_all.27
  159.7 11.0 %all_to_all.32 = s32[16,16,1]{1,2,0:T(1,128)S(1)} all-to-all(s32[16,16,1]{1,2,0:T(1,128)S(1)} %bitcast.34), channel_id=1, replica_groups=mesh['dim'=2,'grp'=16] {'grp'}, dimensions={0} | all-to-all | bytes 2048 | tf_op jit(solution)/shard_map/all_to_all | solution.py:42
  170.8 0.0 copy-done.3
  170.8 6.9 %all-gather.2.cloned.1.call-done = bf16[16,256,1024]{2,1,0:T(8,128)(2,1)} async-done(((bf16[16,256,512]{2,1,0:T(8,128)(2,1)}), bf16[16,256,1024]{2,1,0:T(8,128)(2,1)}) %all-gather.2.cloned.1.call-update) | async-done | bytes 8388624 | tf_op jit(solution)/shard_map/all_gather | solution.py:47
  177.7 0.0 copy-start.1
  177.7 26.0 %add_divide_fusion = f32[16,512,1024]{2,1,0:T(8,128)} fusion(f32[16,512,1024]{2,1,0:T(8,128)} %param.11, f32[16]{0:T(128)S(1)} %add_convert_fusion, bf16[16,256,512]{2,1,0:T(8,128)(2,1)} %bitcast.27, bf16[16,256,1024]{2,1,0:T(8,128)(2,1)} %all-gather.2.cloned.1.call-done), kind=kOutput, calls=%fused_computation.1 | convolution fusion | flops 4311744512 | bytes 79691840 | tf_op jit(solution)/shard_map/lsa,lsb->lab/dot_general | solution.py:44
  203.7 0.0 copy-done.1
  (6 shorter events, 0.1 us)
Async XLA Ops:
  6.5 28.9 %copy-start = (f32[256,512]{1,0:T(8,128)S(1)}, f32[256,512]{1,0:T(8,128)}, u32[]{:S(2)}) copy-start(f32[256,512]{1,0:T(8,128)} %param.8) | copy-start | bytes 1572868
  6.5 28.8 %reduce-scatter.2.cloned.1.call-start = ((), (), s32[]{:S(2)}) async-start(), calls=%async_computation.3 | async-start | bytes 6291456 | tf_op jit(solution)/shard_map/reduce_scatter | solution.py:13
  20.5 0.7 copy-start.2
  20.5 157.2 %all-gather.2.cloned.1.call-start = ((), (), s32[]{:S(2)}) async-start(), calls=%async_computation.4 | async-start | bytes 12582912 | tf_op jit(solution)/shard_map/all_gather | solution.py:47
  159.3 11.4 %copy-start.3 = (s32[16]{0:T(128)S(1)}, s32[16]{0:T(128)}, u32[]{:S(2)}) copy-start(s32[16]{0:T(128)} %param.10) | copy-start | bytes 196
  177.7 26.0 %copy-start.1 = (f32[256,512]{1,0:T(8,128)S(1)}, f32[256,512]{1,0:T(8,128)}, u32[]{:S(2)}) copy-start(f32[256,512]{1,0:T(8,128)} %param.8) | copy-start | bytes 1572868
Sparse Core Ops, SparseCore 0:
  20.6 14.7 reduce-scatter.1
  159.5 18.1 all-gather.1
where the time goes:
time: 211 us
  blocking collectives  112 us (53%)
  matrix products  45.3 us (21%)
  local copies, waits for them, and re-layouts  18.3 us (9%)
  waiting for transfers between devices  17.9 us (8%)
  between operations  13.5 us (6%)
  other arithmetic  3.41 us (2%)
    all_to_all x1, blocking collectives, on_device(): lax.all_to_all(buffer, 'grp', split_axis=0, concat_axis=1, tiled=True)  101 us
    dot_general x1, matrix products, on_device(): jnp.einsum('lsa,lsb->lab', routed, lax.all_gather(routed, 'dim', axis=2,...  26 us
    dot_general x1, matrix products, on_device(): lax.dot_general(pca, states, (((0,), (1,)), ((), ())), preferred_element_...  13.9 us
    scatter x1, local copies, waits for them, and re-layouts, on_device(): jnp.zeros((LISTS * MOST, own_width), jnp.bfloat16).at[slots]  12.6 us
    all_to_all x1, blocking collectives, on_device(): lax.all_to_all(list_counts[:, None], 'grp', split_axis=0, concat_axis=1,...  11 us
    reduce_scatter x1, waiting for transfers between devices, on_device(): lax.psum_scatter(lax.dot_general(pca, states, (((0,), (1,)), ((), ())), p...  10.9 us
    all_gather x1, waiting for transfers between devices, on_device(): lax.all_gather(routed, 'dim', axis=2, tiled=True)  6.91 us
    dot_general x1, matrix products, on_device(): lax.dot_general(centroids, onehot_t, (((0,), (0,)), ((), ())), precision=...  5.32 us
  transfers between devices with their start and end apart: 2, of which 2 were waited for; matrix products, arithmetic and copies ran while one was open for 2% of the time, Pallas kernels for 0%

commit v1 on v0

v1 whole, which is shorter than its diff:
```python
import functools

import jax
import jax.numpy as jnp
from jax import lax
from jax.experimental import pallas as pl
from jax.experimental.pallas import tpu as pltpu
from jax.sharding import PartitionSpec as P

MOST = 16
BLOCK = 256
MESH = pl.DeviceIdType.MESH
CONTRACT_FIRST = (((0,), (0,)), ((), ()))


def route_kernel(
    n, states_hbm, pca_hbm, cent_ref, labels_ref, gath, counts_out,
    states, pca, pieces, to_peer, from_peer, residual, slots, packed, counts,
    states_sem, pca_sem, peer_send, peer_recv, send, recv, pass_send, pass_recv,
    count_send, count_recv, own_sem,
):
    dim, me = lax.axis_index("dim"), lax.axis_index("grp")
    other = 1 - dim
    rows, depth = states.shape
    width = residual.shape[1]
    lists = cent_ref.shape[0]
    cap = packed.shape[1]
    per = lists // n
    blocks = rows // BLOCK

    barrier = pltpu.get_barrier_semaphore()
    pl.semaphore_signal(barrier, inc=1, device_id={"dim": other}, device_id_type=MESH)

    @pl.loop(1, n)
    def _(j):
        pl.semaphore_signal(
            barrier, inc=1, device_id={"grp": lax.rem(me + j, n)}, device_id_type=MESH
        )

    pca_copy = pltpu.make_async_copy(pca_hbm, pca, pca_sem)
    pca_copy.start()

    def states_copy(b):
        at = pl.ds(b * BLOCK, BLOCK)
        return pltpu.make_async_copy(states_hbm.at[at], states.at[at], states_sem.at[b])

    @pl.loop(0, blocks)
    def _(b):
        states_copy(b).start()

    list_of = lax.broadcasted_iota(jnp.int32, (lists, BLOCK), 0)

    def named(b):
        return labels_ref[:, pl.ds(pl.multiple_of(b * BLOCK, BLOCK), BLOCK)] == list_of

    before = (
        lax.broadcasted_iota(jnp.int32, (BLOCK, BLOCK), 0)
        < lax.broadcasted_iota(jnp.int32, (BLOCK, BLOCK), 1)
    ).astype(jnp.float32).astype(jnp.bfloat16)

    def rank_step(b, seen):
        here = named(b)
        onehot = here.astype(jnp.float32)
        earlier = seen + jnp.dot(
            onehot.astype(jnp.bfloat16), before, preferred_element_type=jnp.float32
        )
        ranks = jnp.sum(onehot * earlier, axis=0, keepdims=True).astype(jnp.int32)
        at = pl.ds(pl.multiple_of(b * BLOCK, BLOCK), BLOCK)
        slots[:, at] = labels_ref[:, at] * MOST + ranks
        return seen + jnp.sum(onehot, axis=1, keepdims=True)

    seen = lax.fori_loop(0, blocks, rank_step, jnp.zeros((lists, 1), jnp.float32))
    tallies = jnp.broadcast_to(seen, (lists, 128)).astype(jnp.int32)
    for d in range(n):
        counts[d] = tallies[d * per : (d + 1) * per]

    cent = cent_ref[...]
    high = cent.astype(jnp.bfloat16)
    pieces[0] = high
    rest = cent - high.astype(jnp.float32)
    middle = rest.astype(jnp.bfloat16)
    pieces[1] = middle
    pieces[2] = (rest - middle.astype(jnp.float32)).astype(jnp.bfloat16)

    pl.semaphore_wait(barrier, n)
    pca_copy.wait()

    def peer_copy(b):
        at = pl.ds(pl.multiple_of(b * BLOCK, BLOCK), BLOCK)
        return pltpu.make_async_remote_copy(
            src_ref=to_peer.at[at], dst_ref=from_peer.at[at],
            send_sem=peer_send.at[b], recv_sem=peer_recv.at[b],
            device_id={"dim": other}, device_id_type=MESH,
        )

    def partial(b, part):
        at = pl.ds(pl.multiple_of(b * BLOCK, BLOCK), BLOCK)
        columns = pl.ds(pl.multiple_of(part * width, width), width)
        return jnp.dot(
            states[at, :], pca[:, columns], preferred_element_type=jnp.float32
        ).astype(jnp.bfloat16)

    @pl.loop(0, blocks)
    def _(b):
        states_copy(b).wait()
        to_peer[pl.ds(pl.multiple_of(b * BLOCK, BLOCK), BLOCK), :] = partial(b, other)
        peer_copy(b).start()

    @pl.loop(0, blocks)
    def _(b):
        at = pl.ds(pl.multiple_of(b * BLOCK, BLOCK), BLOCK)
        onehot = named(b).astype(jnp.float32).astype(jnp.bfloat16)
        shift = sum(
            lax.dot_general(
                onehot, pieces[i], CONTRACT_FIRST, preferred_element_type=jnp.float32
            )
            for i in (2, 1, 0)
        )
        own = partial(b, dim).astype(jnp.float32)
        peer_copy(b).wait_recv()
        projected = own + from_peer[at, :].astype(jnp.float32)
        residual[at, :] = (projected - shift).astype(jnp.bfloat16)

    def block_copy(d, source):
        return pltpu.make_async_remote_copy(
            src_ref=packed.at[d], dst_ref=gath.at[dim, source],
            send_sem=send.at[d], recv_sem=recv.at[source],
            device_id={"grp": d}, device_id_type=MESH,
        )

    def count_copy(d, source):
        return pltpu.make_async_remote_copy(
            src_ref=counts.at[d], dst_ref=counts_out.at[source],
            send_sem=count_send.at[d], recv_sem=count_recv.at[source],
            device_id={"grp": d}, device_id_type=MESH,
        )

    def pass_copy(source, half):
        return pltpu.make_async_remote_copy(
            src_ref=gath.at[half, source], dst_ref=gath.at[half, source],
            send_sem=pass_send.at[source], recv_sem=pass_recv.at[source],
            device_id={"dim": other}, device_id_type=MESH,
        )

    slot_of = lax.broadcasted_iota(jnp.int32, (cap, rows), 0)

    @pl.loop(0, n)
    def _(j):
        d = lax.rem(me + n // 2 + j, n)
        chosen = (slots[...] - d * cap == slot_of).astype(jnp.float32).astype(jnp.bfloat16)
        packed[d] = jnp.dot(
            chosen, residual[...], preferred_element_type=jnp.float32
        ).astype(jnp.bfloat16)

        @pl.when(j != n // 2)
        def _():
            block_copy(d, me).start()
            count_copy(d, me).start()

    own_block = pltpu.make_async_copy(packed.at[me], gath.at[dim, me], own_sem.at[0])
    own_count = pltpu.make_async_copy(counts.at[me], counts_out.at[me], own_sem.at[1])
    own_block.start()
    own_count.start()
    own_block.wait()
    own_count.wait()
    pass_copy(me, dim).start()

    @pl.loop(0, n)
    def _(j):
        source = lax.rem(me + n + n // 2 - j, n)

        @pl.when(j != n // 2)
        def _():
            block_copy(source, source).wait_recv()
            pass_copy(source, dim).start()
            count_copy(source, source).wait_recv()

    @pl.loop(0, n)
    def _(j):
        pass_copy(j, dim).wait_send()
        pass_copy(j, other).wait_recv()

    @pl.loop(1, n)
    def _(j):
        d = lax.rem(me + j, n)
        block_copy(d, me).wait_send()
        count_copy(d, me).wait_send()

    @pl.loop(0, blocks)
    def _(b):
        peer_copy(b).wait_send()


def moment_kernel(prior_counts_ref, counts_ref, rows_ref, prior_ref, out_ref):
    dim = lax.axis_index("dim")
    l = pl.program_id(0)
    halves, n, most, width = rows_ref.shape
    total = prior_counts_ref[l] + jnp.sum(counts_ref[:, pl.ds(l, 1), :], axis=0)
    inverse = 1.0 / total.astype(jnp.float32)
    own = rows_ref[dim].reshape(n * most, width)
    for half in range(halves):
        columns = pl.ds(half * width, width)
        gram = lax.dot_general(
            own, rows_ref[half].reshape(n * most, width), CONTRACT_FIRST,
            preferred_element_type=jnp.float32,
        )
        out_ref[0, :, columns] = (prior_ref[0, :, columns] + gram) * inverse[:, :1]


def on_device(n, states, pca, centroids, list_ids, prior_counts, prior_gram):
    rows, depth = states.shape
    lists, width = centroids.shape
    per = lists // n
    cap = per * MOST
    blocks = rows // BLOCK
    dma = pltpu.SemaphoreType.DMA
    vmem = pltpu.VMEM
    any_space = pl.BlockSpec(memory_space=pl.ANY)
    gathered, counts = pl.pallas_call(
        functools.partial(route_kernel, n),
        out_shape=(
            jax.ShapeDtypeStruct((2, n, cap, width), jnp.bfloat16),
            jax.ShapeDtypeStruct((n, per, 128), jnp.int32),
        ),
        in_specs=[
            any_space,
            any_space,
            pl.BlockSpec(memory_space=vmem),
            pl.BlockSpec(memory_space=vmem),
        ],
        out_specs=(any_space, any_space),
        scratch_shapes=[
            vmem((rows, depth), jnp.bfloat16),
            vmem(pca.shape, jnp.bfloat16),
            vmem((3, lists, width), jnp.bfloat16),
            vmem((rows, width), jnp.bfloat16),
            vmem((rows, width), jnp.bfloat16),
            vmem((rows, width), jnp.bfloat16),
            vmem((1, rows), jnp.int32),
            vmem((n, cap, width), jnp.bfloat16),
            vmem((n, per, 128), jnp.int32),
            dma((blocks,)), dma, dma((blocks,)), dma((blocks,)),
            dma((n,)), dma((n,)), dma((n,)), dma((n,)), dma((n,)), dma((n,)), dma((2,)),
        ],
        compiler_params=pltpu.CompilerParams(
            collective_id=0, has_side_effects=True, vmem_limit_bytes=44 * 2**20
        ),
        name="route",
    )(states, pca, centroids, list_ids.reshape(1, rows))
    own = prior_gram.shape[1]
    gram_block = pl.BlockSpec((1, own, 2 * width), lambda l: (l, 0, 0))
    return pl.pallas_call(
        moment_kernel,
        grid=(per,),
        out_shape=jax.ShapeDtypeStruct(prior_gram.shape, jnp.float32),
        in_specs=[
            pl.BlockSpec(memory_space=pltpu.SMEM),
            pl.BlockSpec((n, per, 128), lambda l: (0, 0, 0)),
            pl.BlockSpec((2, n, MOST, width), lambda l: (0, 0, l, 0)),
            gram_block,
        ],
        out_specs=gram_block,
        compiler_params=pltpu.CompilerParams(vmem_limit_bytes=44 * 2**20),
        name="moments",
    )(prior_counts, counts, gathered, prior_gram)


def solution(mesh):
    in_specs = (
        P("grp", "dim"),
        P("dim", None),
        P(None, "dim"),
        P("grp", None),
        P("grp"),
        P("grp", "dim", None),
    )
    return jax.shard_map(
        functools.partial(on_device, mesh.shape["grp"]),
        mesh=mesh,
        in_specs=in_specs,
        out_specs=P("grp", "dim", None),
        check_vma=False,
    )
```

time: 211 us -> 158 us (0.75)
  Pallas kernels: 0 us -> 149 us
  blocking collectives: 112 us -> 0 us
  matrix products: 45.3 us -> 0 us
  waiting for transfers between devices: 17.9 us -> 0 us
  between operations: 13.5 us -> 0.03 us
  local copies, waits for them, and re-layouts: 18.3 us -> 7.32 us
  other arithmetic: 3.41 us -> 0 us
    pallas_call x0 -> x2, Pallas kernels: none -> 149 us  [the longest x1 120 us: on_device(): pl.pallas_call(functools.partial(route_kernel, n), out_shape=(jax.ShapeDt...]
    all_to_all x2 -> x0, blocking collectives: 112 us -> none  [the longest x1 101 us: on_device(): lax.all_to_all(buffer, 'grp', split_axis=0, concat_axis=1, tiled=True)]
    dot_general x3 -> x0, matrix products: 45.3 us -> none  [the longest x1 26 us: on_device(): jnp.einsum('lsa,lsb->lab', routed, lax.all_gather(routed, 'dim', axis=2,...]
    scatter x1 -> x0, local copies, waits for them, and re-layouts: 12.6 us -> none  [on_device(): jnp.zeros((LISTS * MOST, own_width), jnp.bfloat16).at[slots]]
    reduce_scatter x1 -> x0, waiting for transfers between devices: 10.9 us -> none  [on_device(): lax.psum_scatter(lax.dot_general(pca, states, (((0,), (1,)), ((), ())), p...]
    all_gather x1 -> x0, waiting for transfers between devices: 6.91 us -> none  [on_device(): lax.all_gather(routed, 'dim', axis=2, tiled=True)]
    unnamed x8 -> x10, local copies, waits for them, and re-layouts: 0.45 us -> 7.32 us
    reduce_sum x3 -> x0, other arithmetic: 3 us -> none  [the longest x1 2.68 us: on_device(): ranks = jnp.sum(earlier * onehot_int, axis=0)]
  transfers between devices with their start and end apart: 2 -> 0, of which waited for: 2 -> 0; matrix products, arithmetic and copies ran while one was open for 2% -> 0% of each run, Pallas kernels for 0% -> 0%
where the time goes in v1:
time: 158 us; the launch traced here: 156 us
  Pallas kernels  149 us (94%)
  local copies, waits for them, and re-layouts  7.32 us (5%)
    pallas_call x1, Pallas kernels, on_device(): pl.pallas_call(functools.partial(route_kernel, n), out_shape=(jax.ShapeDt...  120 us
    pallas_call x1, Pallas kernels, on_device(): pl.pallas_call(moment_kernel, grid=(per,), out_shape=jax.ShapeDtypeStruct...  29.5 us
    unnamed x10, local copies, waits for them, and re-layouts  7.32 us

profile of v1, /device:TPU:0, one launch (start us, length us, event | category | flops | bytes accessed | tf_op | source)
XLA Modules:
  0.0 156.4 jit_solution(6998597429156415196)
XLA Ops:
  0.0 0.0 copy-start.4
  0.0 0.0 copy-start.1
  0.0 2.2 %copy-done.1 = bf16[2048,1024]{1,0:T(8,128)(2,1)S(1)} copy-done((bf16[2048,1024]{1,0:T(8,128)(2,1)S(1)}, bf16[2048,1024]{1,0:T(8,128)(2,1)}, u32[]{:S(2)}) %copy-start.1) | copy-done | bytes 4194328
  2.2 0.0 copy-start.2
  2.2 1.0 copy-done.2
  3.2 0.0 copy-start.3
  3.2 0.7 copy-done.3
  3.9 119.6 %route.1 = (bf16[2,16,256,512]{3,2,1,0:T(8,128)(2,1)}, s32[16,16,128]{2,1,0:T(8,128)S(1)}) custom-call(bf16[2048,2048]{1,0:T(8,128)(2,1)} %states_hbm.1, bf16[2048,1024]{1,0:T(8,128)(2,1)S(1)} %copy-done.1, f32[256,512]{1,0:T(8,128)S(1)} %copy-done.2, s32[1,2048]{1,0:T(1,128)S(1)} %bitcast.1), custom_call_target="tpu_custom_call" | custom-call | tf_op jit(solution)/shard_map/route/pallas_call | solution.py:219
  123.6 0.0 copy-done.4
  123.6 0.0 copy-start
  123.6 3.4 %copy-done = bf16[2,16,256,512]{3,2,1,0:T(8,128)(2,1)S(1)} copy-done((bf16[2,16,256,512]{3,2,1,0:T(8,128)(2,1)S(1)}, bf16[2,16,256,512]{3,2,1,0:T(8,128)(2,1)}, u32[]{:S(2)}) %copy-start) | copy-done | bytes 8388632
  127.0 29.5 %moments.1 = f32[16,512,1024]{2,1,0:T(8,128)} custom-call(s32[16]{0:T(128)S(1)} %copy-done.4, s32[16,16,128]{2,1,0:T(8,128)S(1)} %get-tuple-element.7.counts_ref, bf16[2,16,256,512]{3,2,1,0:T(8,128)(2,1)S(1)} %copy-done, f32[16,512,1024]{2,1,0:T(8,128)} %prior_ref.1), custom_call_target="tpu_custom_call" | custom-call | tf_op jit(solution)/shard_map/moments/pallas_call | solution.py:252
Async XLA Ops:
  0.0 123.6 %copy-start.4 = (s32[16]{0:T(128)S(1)}, s32[16]{0:T(128)}, u32[]{:S(2)}) copy-start(s32[16]{0:T(128)} %prior_counts_ref.1) | copy-start | bytes 196
  0.0 2.2 %copy-start.1 = (bf16[2048,1024]{1,0:T(8,128)(2,1)S(1)}, bf16[2048,1024]{1,0:T(8,128)(2,1)}, u32[]{:S(2)}) copy-start(bf16[2048,1024]{1,0:T(8,128)(2,1)} %pca_hbm.1) | copy-start | bytes 12582916
  2.2 1.0 copy-start.2
  3.2 0.7 copy-start.3
  123.6 3.4 %copy-start = (bf16[2,16,256,512]{3,2,1,0:T(8,128)(2,1)S(1)}, bf16[2,16,256,512]{3,2,1,0:T(8,128)(2,1)}, u32[]{:S(2)}) copy-start(bf16[2,16,256,512]{3,2,1,0:T(8,128)(2,1)} %get-tuple-element.8.rows_ref) | copy-start | bytes 25165828

commit v2 on v1

v2 whole, which is shorter than its diff:
```python
import functools

import jax
import jax.numpy as jnp
from jax import lax
from jax.experimental import pallas as pl
from jax.experimental.pallas import tpu as pltpu
from jax.sharding import PartitionSpec as P

MOST = 16
BLOCK = 256
PARTS = 2
MESH = pl.DeviceIdType.MESH
CONTRACT_FIRST = (((0,), (0,)), ((), ()))


def route_kernel(
    n, states_hbm, pca_hbm, cent_ref, labels_ref, gath, counts_out,
    states, pca, pieces, to_peer, from_peer, residual, slots, packed, counts,
    states_sem, pca_sem, peer_send, peer_recv, send, recv, pass_send, pass_recv,
    count_send, count_recv, own_sem,
):
    dim, me = lax.axis_index("dim"), lax.axis_index("grp")
    other = 1 - dim
    rows, depth = states.shape
    part = residual.shape[2]
    lists = cent_ref.shape[0]
    cap = packed.shape[2]
    per = lists // n
    blocks = rows // BLOCK

    barrier = pltpu.get_barrier_semaphore()
    pl.semaphore_signal(barrier, inc=1, device_id={"dim": other}, device_id_type=MESH)

    @pl.loop(1, n)
    def _(j):
        pl.semaphore_signal(
            barrier, inc=1, device_id={"grp": lax.rem(me + j, n)}, device_id_type=MESH
        )

    pca_copy = pltpu.make_async_copy(pca_hbm, pca, pca_sem)
    pca_copy.start()

    def states_copy(b):
        at = pl.ds(b * BLOCK, BLOCK)
        return pltpu.make_async_copy(states_hbm.at[at], states.at[at], states_sem.at[b])

    @pl.loop(0, blocks)
    def _(b):
        states_copy(b).start()

    list_of = lax.broadcasted_iota(jnp.int32, (lists, BLOCK), 0)

    def named(b):
        return labels_ref[:, pl.ds(pl.multiple_of(b * BLOCK, BLOCK), BLOCK)] == list_of

    before = (
        lax.broadcasted_iota(jnp.int32, (BLOCK, BLOCK), 0)
        < lax.broadcasted_iota(jnp.int32, (BLOCK, BLOCK), 1)
    ).astype(jnp.float32).astype(jnp.bfloat16)

    def rank_step(b, seen):
        here = named(b)
        onehot = here.astype(jnp.float32)
        earlier = seen + jnp.dot(
            onehot.astype(jnp.bfloat16), before, preferred_element_type=jnp.float32
        )
        ranks = jnp.sum(onehot * earlier, axis=0, keepdims=True).astype(jnp.int32)
        at = pl.ds(pl.multiple_of(b * BLOCK, BLOCK), BLOCK)
        slots[:, at] = labels_ref[:, at] * MOST + ranks
        return seen + jnp.sum(onehot, axis=1, keepdims=True)

    seen = lax.fori_loop(0, blocks, rank_step, jnp.zeros((lists, 1), jnp.float32))
    tallies = jnp.broadcast_to(seen, (lists, 128)).astype(jnp.int32)
    for d in range(n):
        counts[d] = tallies[d * per : (d + 1) * per]

    cent = cent_ref[...]
    high = cent.astype(jnp.bfloat16)
    pieces[0] = high
    rest = cent - high.astype(jnp.float32)
    middle = rest.astype(jnp.bfloat16)
    pieces[1] = middle
    pieces[2] = (rest - middle.astype(jnp.float32)).astype(jnp.bfloat16)

    pl.semaphore_wait(barrier, n)
    pca_copy.wait()

    def rows_at(b):
        return pl.ds(pl.multiple_of(b * BLOCK, BLOCK), BLOCK)

    def peer_copy(q, b):
        return pltpu.make_async_remote_copy(
            src_ref=to_peer.at[q, rows_at(b)], dst_ref=from_peer.at[q, rows_at(b)],
            send_sem=peer_send.at[q * blocks + b], recv_sem=peer_recv.at[q * blocks + b],
            device_id={"dim": other}, device_id_type=MESH,
        )

    def partial(q, b, owner):
        columns = pl.ds(pl.multiple_of((owner * PARTS + q) * part, part), part)
        return jnp.dot(
            states[rows_at(b), :], pca[:, columns], preferred_element_type=jnp.float32
        ).astype(jnp.bfloat16)

    def block_copy(q, d, source):
        return pltpu.make_async_remote_copy(
            src_ref=packed.at[q, d], dst_ref=gath.at[dim * PARTS + q, source],
            send_sem=send.at[q * n + d], recv_sem=recv.at[q * n + source],
            device_id={"grp": d}, device_id_type=MESH,
        )

    def count_copy(d, source):
        return pltpu.make_async_remote_copy(
            src_ref=counts.at[d], dst_ref=counts_out.at[source],
            send_sem=count_send.at[d], recv_sem=count_recv.at[source],
            device_id={"grp": d}, device_id_type=MESH,
        )

    def pass_copy(q, source, half):
        return pltpu.make_async_remote_copy(
            src_ref=gath.at[half * PARTS + q, source], dst_ref=gath.at[half * PARTS + q, source],
            send_sem=pass_send.at[q * n + source], recv_sem=pass_recv.at[q * n + source],
            device_id={"dim": other}, device_id_type=MESH,
        )

    def own_copy(q):
        return pltpu.make_async_copy(
            packed.at[q, me], gath.at[dim * PARTS + q, me], own_sem.at[q]
        )

    own_count = pltpu.make_async_copy(counts.at[me], counts_out.at[me], own_sem.at[PARTS])
    own_count.start()
    slot_of = lax.broadcasted_iota(jnp.int32, (cap, rows), 0)

    for q in range(PARTS):

        @pl.loop(0, blocks)
        def _(b):
            if q == 0:
                states_copy(b).wait()
            to_peer[q, rows_at(b), :] = partial(q, b, other)
            peer_copy(q, b).start()

        @pl.loop(0, blocks)
        def _(b):
            onehot = named(b).astype(jnp.float32).astype(jnp.bfloat16)
            shift = sum(
                lax.dot_general(
                    onehot, pieces[i, :, q * part : (q + 1) * part], CONTRACT_FIRST,
                    preferred_element_type=jnp.float32,
                )
                for i in (2, 1, 0)
            )
            own = partial(q, b, dim).astype(jnp.float32)
            peer_copy(q, b).wait_recv()
            projected = own + from_peer[q, rows_at(b), :].astype(jnp.float32)
            residual[q, rows_at(b), :] = (projected - shift).astype(jnp.bfloat16)

        @pl.loop(0, n)
        def _(j):
            d = lax.rem(me + n // 2 + j, n)
            chosen = (slots[...] - d * cap == slot_of).astype(jnp.float32).astype(jnp.bfloat16)
            packed[q, d] = jnp.dot(
                chosen, residual[q], preferred_element_type=jnp.float32
            ).astype(jnp.bfloat16)

            @pl.when(j != n // 2)
            def _():
                block_copy(q, d, me).start()
                if q == 0:
                    count_copy(d, me).start()

        own_copy(q).start()

    for q in range(PARTS):
        own_copy(q).wait()
        pass_copy(q, me, dim).start()

        @pl.loop(0, n)
        def _(j):
            source = lax.rem(me + n + n // 2 - j, n)

            @pl.when(j != n // 2)
            def _():
                block_copy(q, source, source).wait_recv()
                pass_copy(q, source, dim).start()

    own_count.wait()

    @pl.loop(1, n)
    def _(j):
        d = lax.rem(me + j, n)
        count_copy(d, d).wait_recv()
        count_copy(d, me).wait_send()

    for q in range(PARTS):

        @pl.loop(0, n)
        def _(j):
            pass_copy(q, j, dim).wait_send()
            pass_copy(q, j, other).wait_recv()

        @pl.loop(1, n)
        def _(j):
            block_copy(q, lax.rem(me + j, n), me).wait_send()

        @pl.loop(0, blocks)
        def _(b):
            peer_copy(q, b).wait_send()


def moment_kernel(prior_counts_ref, counts_ref, rows_ref, prior_ref, out_ref):
    dim = lax.axis_index("dim")
    l = pl.program_id(0)
    pieces, n, most, part = rows_ref.shape
    total = prior_counts_ref[l] + jnp.sum(counts_ref[:, pl.ds(l, 1), :], axis=0)
    inverse = 1.0 / total.astype(jnp.float32)
    own = jnp.concatenate(
        [rows_ref[dim * PARTS + q].reshape(n * most, part) for q in range(PARTS)], axis=1
    )
    for piece in range(pieces):
        columns = pl.ds(piece * part, part)
        gram = lax.dot_general(
            own, rows_ref[piece].reshape(n * most, part), CONTRACT_FIRST,
            preferred_element_type=jnp.float32,
        )
        out_ref[0, :, columns] = (prior_ref[0, :, columns] + gram) * inverse[:, :1]


def on_device(n, states, pca, centroids, list_ids, prior_counts, prior_gram):
    rows, depth = states.shape
    lists, width = centroids.shape
    per = lists // n
    cap = per * MOST
    blocks = rows // BLOCK
    part = width // PARTS
    dma = pltpu.SemaphoreType.DMA
    vmem = pltpu.VMEM
    any_space = pl.BlockSpec(memory_space=pl.ANY)
    gathered, counts = pl.pallas_call(
        functools.partial(route_kernel, n),
        out_shape=(
            jax.ShapeDtypeStruct((2 * PARTS, n, cap, part), jnp.bfloat16),
            jax.ShapeDtypeStruct((n, per, 128), jnp.int32),
        ),
        in_specs=[
            any_space,
            any_space,
            pl.BlockSpec(memory_space=vmem),
            pl.BlockSpec(memory_space=vmem),
        ],
        out_specs=(any_space, any_space),
        scratch_shapes=[
            vmem((rows, depth), jnp.bfloat16),
            vmem(pca.shape, jnp.bfloat16),
            vmem((3, lists, width), jnp.bfloat16),
            vmem((PARTS, rows, part), jnp.bfloat16),
            vmem((PARTS, rows, part), jnp.bfloat16),
            vmem((PARTS, rows, part), jnp.bfloat16),
            vmem((1, rows), jnp.int32),
            vmem((PARTS, n, cap, part), jnp.bfloat16),
            vmem((n, per, 128), jnp.int32),
            dma((blocks,)), dma, dma((PARTS * blocks,)), dma((PARTS * blocks,)),
            dma((PARTS * n,)), dma((PARTS * n,)), dma((PARTS * n,)), dma((PARTS * n,)),
            dma((n,)), dma((n,)), dma((PARTS + 1,)),
        ],
        compiler_params=pltpu.CompilerParams(
            collective_id=0, has_side_effects=True, vmem_limit_bytes=60 * 2**20
        ),
        name="route",
    )(states, pca, centroids, list_ids.reshape(1, rows))
    own = prior_gram.shape[1]
    gram_block = pl.BlockSpec((1, own, 2 * width), lambda l: (l, 0, 0))
    return pl.pallas_call(
        moment_kernel,
        grid=(per,),
        out_shape=jax.ShapeDtypeStruct(prior_gram.shape, jnp.float32),
        in_specs=[
            pl.BlockSpec(memory_space=pltpu.SMEM),
            pl.BlockSpec((n, per, 128), lambda l: (0, 0, 0)),
            pl.BlockSpec((2 * PARTS, n, MOST, part), lambda l: (0, 0, l, 0)),
            gram_block,
        ],
        out_specs=gram_block,
        compiler_params=pltpu.CompilerParams(vmem_limit_bytes=60 * 2**20),
        name="moments",
    )(prior_counts, counts, gathered, prior_gram)


def solution(mesh):
    in_specs = (
        P("grp", "dim"),
        P("dim", None),
        P(None, "dim"),
        P("grp", None),
        P("grp"),
        P("grp", "dim", None),
    )
    return jax.shard_map(
        functools.partial(on_device, mesh.shape["grp"]),
        mesh=mesh,
        in_specs=in_specs,
        out_specs=P("grp", "dim", None),
        check_vma=False,
    )
```

time: 158 us -> 146 us (0.924)
  local copies, waits for them, and re-layouts: 7.32 us -> 0 us
  Pallas kernels: 149 us -> 146 us
    unnamed x10 -> x0, local copies, waits for them, and re-layouts: 7.32 us -> none
    pallas_call x1, Pallas kernels: 120 us -> 114 us  [on_device(): pl.pallas_call(functools.partial(route_kernel, n), out_shape=(jax.ShapeDt...]
    pallas_call x1, Pallas kernels: 29.5 us -> 31.2 us  [on_device(): pl.pallas_call(moment_kernel, grid=(per,), out_shape=jax.ShapeDtypeStruct...]
where the time goes in v2:
time: 146 us
  Pallas kernels  146 us (100%)
    pallas_call x1, Pallas kernels, on_device(): pl.pallas_call(functools.partial(route_kernel, n), out_shape=(jax.ShapeDt...  114 us
    pallas_call x1, Pallas kernels, on_device(): pl.pallas_call(moment_kernel, grid=(per,), out_shape=jax.ShapeDtypeStruct...  31.2 us

profile of v2, /device:TPU:0, one launch (start us, length us, event | category | flops | bytes accessed | tf_op | source)
XLA Modules:
  0.0 145.6 jit_solution(6403690787872484077)
XLA Ops:
  0.0 114.4 %route.1 = (bf16[4,16,256,256]{3,2,1,0:T(8,128)(2,1)}, s32[16,16,128]{2,1,0:T(8,128)}) custom-call(bf16[2048,2048]{1,0:T(8,128)(2,1)} %states_hbm.1, bf16[2048,1024]{1,0:T(8,128)(2,1)} %pca_hbm.1, f32[256,512]{1,0:T(8,128)} %cent_ref.1, s32[1,2048]{1,0:T(1,128)} %bitcast.1), custom_call_target="tpu_custom_call" | custom-call | tf_op jit(solution)/shard_map/route/pallas_call | solution.py:240
  114.4 31.2 %moments.1 = f32[16,512,1024]{2,1,0:T(8,128)} custom-call(s32[16]{0:T(128)} %prior_counts_ref.1, s32[16,16,128]{2,1,0:T(8,128)} %get-tuple-element.7.counts_ref, bf16[4,16,256,256]{3,2,1,0:T(8,128)(2,1)} %get-tuple-element.8.rows_ref, f32[16,512,1024]{2,1,0:T(8,128)} %prior_ref.1), custom_call_target="tpu_custom_call" | custom-call | tf_op jit(solution)/shard_map/moments/pallas_call | solution.py:274

commit v3 on v2

--- a/solution.py
+++ b/solution.py
@@ -216,13 +216,12 @@
     total = prior_counts_ref[l] + jnp.sum(counts_ref[:, pl.ds(l, 1), :], axis=0)
     inverse = 1.0 / total.astype(jnp.float32)
     own = jnp.concatenate(
-        [rows_ref[dim * PARTS + q].reshape(n * most, part) for q in range(PARTS)], axis=1
+        [rows_ref[dim * PARTS + q].reshape(n * most, part).T for q in range(PARTS)], axis=0
     )
     for piece in range(pieces):
         columns = pl.ds(piece * part, part)
-        gram = lax.dot_general(
-            own, rows_ref[piece].reshape(n * most, part), CONTRACT_FIRST,
-            preferred_element_type=jnp.float32,
+        gram = jnp.dot(
+            own, rows_ref[piece].reshape(n * most, part), preferred_element_type=jnp.float32
         )
         out_ref[0, :, columns] = (prior_ref[0, :, columns] + gram) * inverse[:, :1]
 

time: 146 us -> 146 us (level)
  no operation moved by 1% of the time
where the time goes in v3:
time: 146 us
  Pallas kernels  146 us (100%)
    pallas_call x1, Pallas kernels, on_device(): pl.pallas_call(functools.partial(route_kernel, n), out_shape=(jax.ShapeDt...  114 us
    pallas_call x1, Pallas kernels, on_device(): pl.pallas_call(moment_kernel, grid=(per,), out_shape=jax.ShapeDtypeStruct...  31.2 us

profile of v3, /device:TPU:0, one launch (start us, length us, event | category | flops | bytes accessed | tf_op | source)
XLA Modules:
  0.0 145.6 jit_solution(6403690787872484077)
XLA Ops:
  0.0 114.4 %route.1 = (bf16[4,16,256,256]{3,2,1,0:T(8,128)(2,1)}, s32[16,16,128]{2,1,0:T(8,128)}) custom-call(bf16[2048,2048]{1,0:T(8,128)(2,1)} %states_hbm.1, bf16[2048,1024]{1,0:T(8,128)(2,1)} %pca_hbm.1, f32[256,512]{1,0:T(8,128)} %cent_ref.1, s32[1,2048]{1,0:T(1,128)} %bitcast.1), custom_call_target="tpu_custom_call" | custom-call | tf_op jit(solution)/shard_map/route/pallas_call | solution.py:239
  114.4 31.2 %moments.1 = f32[16,512,1024]{2,1,0:T(8,128)} custom-call(s32[16]{0:T(128)} %prior_counts_ref.1, s32[16,16,128]{2,1,0:T(8,128)} %get-tuple-element.7.counts_ref, bf16[4,16,256,256]{3,2,1,0:T(8,128)(2,1)} %get-tuple-element.8.rows_ref, f32[16,512,1024]{2,1,0:T(8,128)} %prior_ref.1), custom_call_target="tpu_custom_call" | custom-call | tf_op jit(solution)/shard_map/moments/pallas_call | solution.py:273
